TPU v7x, 512 devices: a whole 4x8x8 slice. The times are simulated.
512 devices in a mesh: branch: 32 (over z_hi, x, core), fsdp: 16 (over z_lo, y).
Axes of the slice: x: 4, y: 8, z: 8 (z_hi: 4, z_lo: 2; z = z_hi * 2 + z_lo), core: 2. Of those that a mesh axis runs over, the one named last changes fastest.
Arguments:
- activations: bfloat16 [32, 512, 192], P('branch', 'fsdp'), may hold values from -16 to 16
- weights: bfloat16 [32, 192, 29568], P('branch', None, 'fsdp'), may hold values from -6 to 6
- output_grads: bfloat16 [32, 512, 29568], P('branch', None, 'fsdp'), may hold values from -16 to 16
Outputs:
- merged: bfloat16 [192, 29568], P(None, 'fsdp')
- mean_fisher: float32 [192, 29568], P(None, 'fsdp')
All inputs are finite; a program needn't handle non-finite values.
Results may differ from a plain program's by a relative error of at most 0.0038.
Values may be sent and summed in bfloat16 or wider, within the bound.
A program may use at most 64 MiB of HBM per device.

v0:
```python
import jax
import jax.numpy as jnp
from jax import lax
from jax.sharding import Mesh
from jax.sharding import PartitionSpec as P

BRANCH = ("branch_0", "branch_1", "branch_2")


def sent_to_all(x, axis):
    devices = lax.axis_size(axis)
    return lax.all_to_all(jnp.broadcast_to(x[None], (devices, *x.shape)), axis, 0, 0, tiled=True)


def joined_along(parts, dim):
    parts = jnp.moveaxis(parts, 0, dim)
    lengths = parts.shape
    return parts.reshape(*lengths[:dim], lengths[dim] * lengths[dim + 1], *lengths[dim + 2 :])


def collect(x, axis, dim):
    parts = sent_to_all(x, axis)
    return joined_along(parts, dim)


def rows_for(lines, devices):
    spare = -len(lines) % devices
    return jnp.pad(lines, [(0, spare)] + [(0, 0)] * (lines.ndim - 1))


def gather_axes(x, axes, dim):
    far, near = axes
    parts = sent_to_all(sent_to_all(x, far), near)
    return joined_along(parts.swapaxes(0, 1).reshape(-1, *x.shape), dim)


def split_up(x, dim, devices):
    lengths = x.shape
    parts = x.reshape(*lengths[:dim], devices, lengths[dim] // devices, *lengths[dim + 1 :])
    return jnp.moveaxis(parts, dim, 0)


def sum_at_owner(x, axis, dim):
    devices = lax.axis_size(axis)
    parts = lax.all_to_all(split_up(x, dim, devices), axis, 0, 0, tiled=True)
    return jnp.sum(parts, axis=0)


def summed_rows(x, axes, dim):
    far, near = axes
    own = sum_at_owner(split_up(x, dim, lax.axis_size(far)), near, dim + 1)
    return jnp.sum(lax.all_to_all(own, far, 0, 0, tiled=True), axis=0)


def nested_sum(x, axes):
    padded = rows_for(x, lax.axis_size(axes[0]) * lax.axis_size(axes[1]))
    whole = gather_axes(summed_rows(padded, axes, 0), axes, 0)
    return lax.slice_in_dim(whole, 0, len(x)).reshape(x.shape)


def packed_total(arrays, axis):
    ends = [0]
    for a in arrays:
        ends.append(ends[-1] + a.size)
    so_far = nested_sum(jnp.concatenate([a.ravel() for a in arrays]), axis)
    return tuple((so_far[b:e].reshape(a.shape) for a, b, e in zip(arrays, ends, ends[1:])))


def on_device(activations, weights, output_grads):
    local_w = weights[0]
    total_tokens = output_grads.shape[1]
    grad_f = output_grads[0].astype(jnp.float32)
    grad_sq = (grad_f * grad_f).astype(jnp.bfloat16)
    act_f = collect(activations, "fsdp", 1)[0].astype(jnp.float32)
    act_sq = (act_f * act_f).astype(jnp.bfloat16)
    fisher = (
        lax.dot_general(
            act_sq, grad_sq, (((0,), (0,)), ((), ())), preferred_element_type=jnp.float32
        )
        / total_tokens
    )
    weighted = fisher * local_w.astype(jnp.float32)
    count_branches = lax.axis_size(BRANCH)
    total_weighted, total_fisher = packed_total(
        (weighted, fisher), (("branch_0", "branch_1"), "branch_2")
    )
    merged = (total_weighted / (total_fisher + 1e-06)).astype(jnp.bfloat16)
    mean_fisher = total_fisher / count_branches
    return (merged, mean_fisher)


def solution(mesh):
    torus = Mesh(
        mesh.devices.reshape(4, 4, 2, mesh.shape["fsdp"]),
        ("branch_0", "branch_1", "branch_2", "fsdp"),
    )
    placed = (P(BRANCH, "fsdp", None), P(BRANCH, None, "fsdp"), P(BRANCH, None, "fsdp"))
    return jax.shard_map(
        on_device,
        mesh=torus,
        in_specs=placed,
        out_specs=(P(None, "fsdp"), P(None, "fsdp")),
        check_vma=False,
    )
```

profile of v0, /device:TPU:57, one launch (start us, length us, event | category | flops | bytes accessed | tf_op | source)
XLA Modules:
  0.0 145.5 jit_solution(1491599058732246670)
XLA Ops:
  0.6 0.0 copy-start.1
  0.6 0.8 broadcast_in_dim.11
  1.5 16.4 %all_to_all.30 = bf16[16,1,32,192]{3,2,1,0:T(8,128)(2,1)S(1)} all-to-all(bf16[16,1,32,192]{3,2,1,0:T(8,128)(2,1)S(1)} %broadcast_in_dim.11), channel_id=1, replica_groups=mesh['branch_0'=4,'branch_1'=4,'branch_2'=2,'fsdp'=16] {'fsdp'}, dimensions={0} | all-to-all | bytes 393216 | tf_op jit(solution)/shard_map/all_to_all | solution.py:12
  17.9 0.0 copy-done.1
  17.9 2.3 %convert_multiply_fusion = (f32[192,1848]{1,0:T(8,128)S(1)}, f32[192,1848]{1,0:T(8,128)S(1)}) fusion(bf16[1,192,1848]{2,1,0:T(8,128)(2,1)S(1)} %copy-done.1, bf16[512,192]{1,0:T(8,128)(2,1)S(1)} %bitcast.19, bf16[1,512,1848]{1,2,0:T(8,128)(2,1)} %param.5), kind=kOutput, calls=%fused_computation.4 | convolution fusion | flops 367234560 | bytes 5637120 | tf_op jit(solution)/shard_map/dot_general | solution.py:77
  20.2 2.9 %concatenate.8 = f32[8,2,22176]{2,1,0:T(2,128)} reshape(f32[192,1848]{1,0:T(8,128)S(1)} %get-tuple-element.4) | data formatting | bytes 2838528 | tf_op jit(solution)/shard_map/concatenate | solution.py:65
  23.2 2.6 %copy.7 = f32[8,2,22176]{2,0,1:T(8,128)} copy(f32[8,2,22176]{2,1,0:T(2,128)} %concatenate.8) | data formatting | bytes 2838528 | tf_op jit(solution)/shard_map/concatenate | solution.py:65
  25.7 1.8 %concatenate.9 = f32[8,2,22176]{2,1,0:T(2,128)S(1)} reshape(f32[192,1848]{1,0:T(8,128)S(1)} %get-tuple-element.5) | data formatting | bytes 2838528 | tf_op jit(solution)/shard_map/concatenate | solution.py:65
  27.5 0.0 copy-start
  27.5 0.1 copy.8
  27.6 1.2 copy-done
  28.9 0.2 maximum_bitcast_fusion
  29.1 7.9 %all_to_all.31 = f32[2,16,22176]{2,1,0:T(8,128)S(1)} all-to-all(f32[2,16,22176]{2,1,0:T(8,128)S(1)} %maximum_bitcast_fusion), channel_id=1, replica_groups=mesh['branch_0'=4,'branch_1'=4,'branch_2'=2,'fsdp'=16] {'branch_2'}, dimensions={0} | all-to-all | bytes 5677056 | tf_op jit(solution)/shard_map/all_to_all | solution.py:45
  36.9 1.4 reduce_sum.18
  38.4 2.3 %all_to_all.21 = f32[16,1,22176]{2,1,0:T(1,128)S(1)} reshape(f32[16,22176]{1,0:T(8,128)} %reduce_sum.18) | data formatting | bytes 2838528 | tf_op jit(solution)/shard_map/all_to_all | solution.py:52
  40.7 45.4 %all_to_all.32 = f32[16,1,22176]{2,1,0:T(1,128)S(1)} all-to-all(f32[16,1,22176]{2,1,0:T(1,128)S(1)} %all_to_all.21), channel_id=1, replica_groups=mesh['branch_0'=4,'branch_1'=4,'branch_2'=2,'fsdp'=16] {'branch_0','bran..., dimensions={0} | all-to-all | bytes 2838528 | tf_op jit(solution)/shard_map/all_to_all | solution.py:52
  86.1 0.9 reduce_sum.19
  87.0 0.7 broadcast_in_dim.24
  87.7 43.9 %all_to_all.33 = f32[16,1,22176]{2,1,0:T(1,128)S(1)} all-to-all(f32[16,1,22176]{2,1,0:T(1,128)S(1)} %broadcast_in_dim.24), channel_id=1, replica_groups=mesh['branch_0'=4,'branch_1'=4,'branch_2'=2,'fsdp'=16] {'branch_0','bran..., dimensions={0} | all-to-all | bytes 2838528 | tf_op jit(solution)/shard_map/all_to_all | solution.py:12
  131.7 0.1 copy.13
  131.8 0.2 broadcast_in_dim.26
  132.0 6.9 %all_to_all.34 = f32[2,16,22176]{2,1,0:T(8,128)S(1)} all-to-all(f32[2,16,22176]{2,1,0:T(8,128)S(1)} %broadcast_in_dim.26), channel_id=1, replica_groups=mesh['branch_0'=4,'branch_1'=4,'branch_2'=2,'fsdp'=16] {'branch_2'}, dimensions={0} | all-to-all | bytes 5677056 | tf_op jit(solution)/shard_map/all_to_all | solution.py:12
  138.8 0.2 slice_multiply_fusion
  139.1 0.7 copy.10
  139.8 3.1 %div.23 = f32[192,1848]{1,0:T(8,128)} reshape(f32[8,2,22176]{2,1,0:T(2,128)S(1)} %copy.10) | data formatting | bytes 2838528 | tf_op jit(solution)/shard_map/div | solution.py:88
  142.9 0.6 copy.9
  143.4 2.1 %convert_element_type.41 = bf16[192,1848]{1,0:T(8,128)(2,1)} reshape(bf16[8,2,22176]{2,1,0:T(2,128)(2,1)S(1)} %copy.9) | data formatting | bytes 1419264 | tf_op jit(solution)/shard_map/convert_element_type | solution.py:87
  (1 shorter events, 0.0 us)
Async XLA Ops:
  0.6 17.3 %copy-start.1 = (bf16[1,192,1848]{2,1,0:T(8,128)(2,1)S(1)}, bf16[1,192,1848]{2,1,0:T(8,128)(2,1)}, u32[]{:S(2)}) copy-start(bf16[1,192,1848]{2,1,0:T(8,128)(2,1)} %param.4) | copy-start | bytes 2128900
  27.5 1.4 copy-start
where the time goes:
time: 146 us
  blocking collectives  120 us (82%)
  local copies, waits for them, and re-layouts  19.2 us (13%)
  other arithmetic  2.74 us (2%)
  matrix products  2.35 us (2%)
    all_to_all x3, blocking collectives, sent_to_all(): lax.all_to_all(jnp.broadcast_to(x[None], (devices, *x.shape)), axis, 0, 0...  67.2 us
    all_to_all x1, blocking collectives, summed_rows(): return jnp.sum(lax.all_to_all(own, far, 0, 0, tiled=True), axis=0)  45.4 us
    all_to_all x1, blocking collectives, sum_at_owner(): parts = lax.all_to_all(split_up(x, dim, devices), axis, 0, 0, tiled=True)  7.86 us
    concatenate x4, local copies, waits for them, and re-layouts, packed_total(): so_far = nested_sum(jnp.concatenate([a.ravel() for a in arrays]), axis)  7.38 us
    div x2, local copies, waits for them, and re-layouts, on_device(): mean_fisher = total_fisher / count_branches  3.82 us

commit v1 on v0

v1 whole, which is shorter than its diff:
```python
import functools

import jax
import jax.numpy as jnp
from jax import lax
from jax.experimental import pallas as pl
from jax.experimental.pallas import tpu as pltpu
from jax.sharding import PartitionSpec as P

MESH = pl.DeviceIdType.MESH
F32, BF16 = jnp.float32, jnp.bfloat16
ROWS, FF, TOK, OWN = 192, 1848, 512, 32
FS = TOK // OWN
RX, CZ, HALF = ROWS // 4, 256, 1024
AHEAD = (2, 1, 3, 0)


def kernel(
    act_hbm, w_hbm, g_hbm, mf,
    act_v, g_full, w_full, g_tail, w_tail, g_in, w_in, sq, wt, pack, at,
    acc, snd, rx, zs, zrx,
    load_sem, g_s, g_r, a_s, a_r, f_s, f_r, x_s, x_r, z_s, z_r,
    agz_s, agz_r, agx_s, agx_r, agc_s, agc_r,
):
    b, fs = lax.axis_index("branch"), lax.axis_index("fsdp")
    zh, x, c = b // 8, lax.rem(b // 2, 4), lax.rem(b, 2)
    zl, y = fs // 8, lax.rem(fs, 8)

    def dev(zh=zh, x=x, c=c, fs=fs):
        return (zh * 8 + x * 2 + c, fs)

    other = dev(c=1 - c)
    steps = sorted(((dy, dz) for dy in range(8) for dz in range(2) if dy or dz), key=lambda s: -(min(s[0], 8 - s[0]) + s[1]))
    mates = [lax.rem(zl + dz, 2) * 8 + lax.rem(y + dy, 8) for dy, dz in steps]
    senders = [lax.rem(zl + dz, 2) * 8 + lax.rem(y + 8 - dy, 8) for dy, dz in steps]
    xs = {d: lax.rem(x + d, 4) for d in range(4)}
    zs_to = [lax.rem(zh + d, 4) for d in AHEAD]

    loads = [
        pltpu.make_async_copy(act_hbm.at[0], act_v, load_sem.at[0]),
        pltpu.make_async_copy(g_hbm.at[0], g_full, load_sem.at[1]),
        pltpu.make_async_copy(w_hbm.at[0], w_full, load_sem.at[2]),
    ]
    for cp in loads:
        cp.start()
    barrier = pltpu.get_barrier_semaphore()
    partners = [dev(fs=m) for m in mates] + [other] + [dev(x=xs[d]) for d in (1, 2, 3)] + [dev(zh=q) for q in zs_to[:3]]
    for p in partners:
        pl.semaphore_signal(barrier, inc=1, device_id=p, device_id_type=MESH)

    loads[0].wait()
    a = act_v[...]
    a = a * a
    pack[0, fs, 0:32, :] = a[:, 0:128]
    pack[0, fs, 32:48, 0:64] = a[0:16, 128:192]
    pack[0, fs, 32:48, 64:128] = a[16:32, 128:192]
    loads[1].wait()
    loads[2].wait()
    g_tail[...] = jnp.zeros_like(g_tail)
    w_tail[...] = jnp.zeros_like(w_tail)
    g_tail[:, 0:56] = g_full[:, 1792:1848]
    w_tail[:, 0:56] = w_full[:, 1792:1848]

    pl.semaphore_wait(barrier, len(partners))

    def remote(src, dst, s, r, to):
        return pltpu.make_async_remote_copy(src_ref=src, dst_ref=dst, send_sem=s, recv_sem=r, device_id=to, device_id_type=MESH)

    sent = []
    for i, m in enumerate(mates):
        cp = remote(pack.at[0, fs], pack.at[0, fs], a_s.at[i], a_r.at[i], dev(fs=m))
        cp.start()
        sent.append(cp)

    def push(gs, ws):
        for i in range(2):
            lo, hi = (0, 768) if i == 0 else (768, 1024)
            remote(gs[i], g_in.at[:, lo:hi], g_s.at[i], g_r.at[i], other).start()
            remote(ws[i], w_in.at[:, lo:hi], g_s.at[2 + i], g_r.at[2 + i], other).start()

    @pl.when(c == 0)
    def _():
        push((g_full.at[:, 1024:1792], g_tail), (w_full.at[:, 1024:1792], w_tail))

    @pl.when(c == 1)
    def _():
        push((g_full.at[:, 0:768], g_full.at[:, 768:1024]), (w_full.at[:, 0:768], w_full.at[:, 768:1024]))

    def square(slot, k, g):
        g = g * g
        g = g.reshape(FS, 2, 16, CZ)
        for h in range(2):
            sq[slot, k, 256 * h : 256 * h + 256, :] = g[:, h].reshape(256, CZ)

    for cc in range(2):

        @pl.when(c == cc)
        def _():
            for k in range(4):
                lo = cc * HALF + k * CZ
                if lo + CZ <= FF:
                    square(0, k, g_full[:, lo : lo + CZ])
                    wt[0, k] = w_full[:, lo : lo + CZ]
                else:
                    square(0, k, g_tail[...])
                    wt[0, k] = w_tail[...]

    pushed = []
    for i in range(2):
        lo, hi = (0, 768) if i == 0 else (768, 1024)
        pushed.append(remote(g_in.at[:, lo:hi], g_in.at[:, lo:hi], g_s.at[i], g_r.at[i], other))
        pushed.append(remote(w_in.at[:, lo:hi], w_in.at[:, lo:hi], g_s.at[2 + i], g_r.at[2 + i], other))
    for cp in pushed:
        cp.wait_recv()
    for k in range(4):
        square(1, k, g_in[:, k * CZ : (k + 1) * CZ])
        wt[1, k] = w_in[:, k * CZ : (k + 1) * CZ]

    fwd = []

    def pass_on(i, blk):
        cp = remote(pack.at[0, blk], pack.at[1, blk], f_s.at[i], f_r.at[i], other)
        cp.start()
        fwd.append(cp)

    pass_on(15, fs)
    for i in reversed(range(15)):
        sent[i].wait_recv()
        pass_on(i, senders[i])

    def turn(slot):
        p = pack[slot]
        left = jnp.concatenate([p[:, 0:16].reshape(256, 128), p[:, 16:32].reshape(256, 128)], axis=0)
        at[slot, 0:128, :] = left.T
        right = p[:, 32:48].reshape(256, 128).T
        at[slot, 128:192, 0:256] = right[0:64]
        at[slot, 128:192, 256:512] = right[64:128]

    turn(0)
    for cp in fwd:
        cp.wait_recv()
    turn(1)

    xcopies = []
    for j in range(4):
        k = zs_to[j]
        f0 = jnp.dot(at[0], sq[0, k], preferred_element_type=F32)
        f1 = jnp.dot(at[1], sq[1, k], preferred_element_type=F32)
        tf = f0 + f1
        tw = f0 * wt[0, k].astype(F32) + f1 * wt[1, k].astype(F32)
        for r in range(4):
            rows = slice(r * RX, r * RX + RX)
            acc[j, r, 0], acc[j, r, 1] = tf[rows], tw[rows]
            snd[j, r, 0], snd[j, r, 1] = tf[rows].astype(BF16), tw[rows].astype(BF16)
        row = []
        for d in (2, 1, 3):
            cp = remote(snd.at[j, xs[d]], rx.at[j, d - 1], x_s.at[j, d - 1], x_r.at[j, d - 1], dev(x=xs[d]))
            cp.start()
            row.append(cp)
        xcopies.append(row)

    zcopies = []
    for j in range(4):
        for cp in xcopies[j]:
            cp.wait_recv()
        s = acc[j, x] + rx[j, 0].astype(F32) + rx[j, 1].astype(F32) + rx[j, 2].astype(F32)
        if j < 3:
            zs[j] = s.astype(BF16)
            cp = remote(zs.at[j], zrx.at[j], z_s.at[j], z_r.at[j], dev(zh=zs_to[j]))
            cp.start()
            zcopies.append(cp)
    for j in (1, 2, 0):
        zcopies[j].wait_recv()
        s = s + zrx[j].astype(F32)
    s = s * (1.0 / TOK)
    tf, tw = s[0], s[1]

    def block(x, zh, c=c):
        return mf.at[:, pl.ds(pl.multiple_of(x * RX, 16), RX), pl.ds(pl.multiple_of(c * HALF + zh * CZ, CZ), CZ)]

    own = block(x, zh)
    own[0] = (tw / (tf + 1e-6)).astype(BF16)
    own[1] = (tf * (1.0 / 32)).astype(BF16)

    agz, agx, agc = [], {}, []

    def along_x(j, z):
        for d in (2, 1, 3):
            blk = block(x, z)
            cp = remote(blk, blk, agx_s.at[j, d - 1], agx_r.at[j, d - 1], dev(x=xs[d]))
            cp.start()
            agx[j, d] = cp

    def across(xx, z):
        i = len(agc)
        blk = block(xx, z)
        cp = remote(blk, blk, agc_s.at[i], agc_r.at[i], other)
        cp.start()
        agc.append(cp)

    for j in range(3):
        cp = remote(own, own, agz_s.at[j], agz_r.at[j], dev(zh=zs_to[j]))
        cp.start()
        agz.append(cp)
    along_x(3, zh)
    across(x, zh)
    zfrom = {j: lax.rem(zh + 4 - AHEAD[j], 4) for j in range(4)}
    for j in (1, 2, 0):
        agz[j].wait_recv()
        along_x(j, zfrom[j])
        across(x, zfrom[j])
    for j in (3, 1, 2, 0):
        for d in (1, 3, 2):
            agx[j, d].wait_recv()
            across(lax.rem(x + 4 - d, 4), zfrom[j])
    for cp in agc:
        cp.wait_recv()
    for cp in sent + pushed + fwd + sum(xcopies, []) + zcopies + agz + list(agx.values()) + agc:
        cp.wait_send()


def on_device(activations, weights, output_grads):
    dma = pltpu.SemaphoreType.DMA
    mf = pl.pallas_call(
        kernel,
        out_shape=jax.ShapeDtypeStruct((2, ROWS, 2 * HALF), BF16),
        in_specs=[pl.BlockSpec(memory_space=pl.ANY)] * 3,
        out_specs=pl.BlockSpec(memory_space=pltpu.VMEM),
        scratch_shapes=[
            pltpu.VMEM((OWN, ROWS), BF16),
            pltpu.VMEM((TOK, FF), BF16),
            pltpu.VMEM((ROWS, FF), BF16),
            pltpu.VMEM((TOK, CZ), BF16),
            pltpu.VMEM((ROWS, CZ), BF16),
            pltpu.VMEM((TOK, HALF), BF16),
            pltpu.VMEM((ROWS, HALF), BF16),
            pltpu.VMEM((2, 4, TOK, CZ), BF16),
            pltpu.VMEM((2, 4, ROWS, CZ), BF16),
            pltpu.VMEM((2, FS, 48, 128), BF16),
            pltpu.VMEM((2, ROWS, TOK), BF16),
            pltpu.VMEM((4, 4, 2, RX, CZ), F32),
            pltpu.VMEM((4, 4, 2, RX, CZ), BF16),
            pltpu.VMEM((4, 3, 2, RX, CZ), BF16),
            pltpu.VMEM((3, 2, RX, CZ), BF16),
            pltpu.VMEM((3, 2, RX, CZ), BF16),
            dma((3,)), dma((4,)), dma((4,)), dma((15,)), dma((15,)), dma((16,)), dma((16,)),
            dma((4, 3)), dma((4, 3)), dma((3,)), dma((3,)),
            dma((3,)), dma((3,)), dma((4, 3)), dma((4, 3)), dma((16,)), dma((16,)),
        ],
        compiler_params=pltpu.CompilerParams(collective_id=0, has_side_effects=True, vmem_limit_bytes=40 << 20),
        name="merge",
    )(activations, weights, output_grads)
    return mf[0, :, :FF], mf[1, :, :FF].astype(F32)


def solution(mesh):
    placed = (P("branch", "fsdp", None), P("branch", None, "fsdp"), P("branch", None, "fsdp"))
    return jax.shard_map(
        on_device, mesh=mesh, in_specs=placed, out_specs=(P(None, "fsdp"), P(None, "fsdp")), check_vma=False
    )
```

time: 146 us -> 60.3 us (0.41)
  the two profiles are of different devices: /device:TPU:57 before, /device:TPU:1 now
where the time goes in v1:
time: 60.3 us; the launch traced here: 60.1 us
  Pallas kernels  55.1 us (91%)
  local copies, waits for them, and re-layouts  2.85 us (5%)
  other arithmetic  1.52 us (3%)
  between operations  0.68 us (1%)
    pallas_call x1, Pallas kernels, on_device(): pl.pallas_call(kernel, out_shape=jax.ShapeDtypeStruct((2, ROWS, 2 * HALF)...  55.1 us
    unnamed x5, local copies, waits for them, and re-layouts  2.85 us
    convert_element_type x1, other arithmetic, on_device(): return (mf[0, :, :FF], mf[1, :, :FF].astype(F32))  1.52 us

profile of v1, /device:TPU:1, one launch (start us, length us, event | category | flops | bytes accessed | tf_op | source)
XLA Modules:
  0.0 60.1 jit_solution(17401201153553106333)
XLA Ops:
  0.6 0.0 copy-start
  0.6 0.0 copy-start.1
  0.6 2.8 %copy.5.g_hbm = bf16[1,512,1848]{2,1,0:T(8,128)(2,1)S(1)} copy(bf16[1,512,1848]{1,2,0:T(8,128)(2,1)} %param.5) | data formatting | bytes 3784704 | tf_op args[2]
  3.5 0.0 copy-done
  3.5 0.0 copy-done.1
  3.5 55.1 %merge.1 = bf16[2,192,2048]{2,1,0:T(8,128)(2,1)S(1)} custom-call(bf16[1,32,192]{2,1,0:T(8,128)(2,1)S(1)} %copy-done.1, bf16[1,192,1848]{2,1,0:T(8,128)(2,1)S(1)} %copy-done, bf16[1,512,1848]{2,1,0:T(8,128)(2,1)S(1)} %copy.5.g_hbm), custom_call_target="tpu_custom_call" | custom-call | tf_op jit(solution)/shard_map/merge/pallas_call | solution.py:224
  58.6 1.5 %bitcast_convert_fusion = (f32[192,1848]{1,0:T(8,128)}, bf16[192,1848]{1,0:T(8,128)(2,1)}) fusion(bf16[2,192,2048]{2,1,0:T(8,128)(2,1)S(1)} %merge.1), kind=kLoop, calls=%fused_computation | loop fusion | flops 354816 | bytes 3548160 | tf_op jit(solution)/shard_map/convert_element_type | solution.py:253
Async XLA Ops:
  0.6 2.9 %copy-start = (bf16[1,192,1848]{2,1,0:T(8,128)(2,1)S(1)}, bf16[1,192,1848]{2,1,0:T(8,128)(2,1)}, u32[]{:S(2)}) copy-start(bf16[1,192,1848]{2,1,0:T(8,128)(2,1)} %w_hbm.1) | copy-start | bytes 2128900
  0.6 2.9 %copy-start.1 = (bf16[1,32,192]{2,1,0:T(8,128)(2,1)S(1)}, bf16[1,32,192]{2,1,0:T(8,128)(2,1)}, u32[]{:S(2)}) copy-start(bf16[1,32,192]{2,1,0:T(8,128)(2,1)} %act_hbm.1) | copy-start | bytes 36868
